TPU v7x, 512 devices: a whole 4x8x8 slice. The times are simulated.
512 devices in a mesh: contrast: 16 (over z, x_lo), dp: 32 (over x_hi, y, core).
Axes of the slice: x: 4 (x_hi: 2, x_lo: 2; x = x_hi * 2 + x_lo), y: 8, z: 8, core: 2. Of those that a mesh axis runs over, the one named last changes fastest.
Arguments:
- image_emb: bfloat16 [262144, 1152], P(('dp', 'contrast')), parts along dimension 0, may hold values from -0.17675781 to 0.17675781
- text_emb: bfloat16 [262144, 1152], P(('dp', 'contrast')), parts along dimension 0, may hold values from -0.17675781 to 0.17675781
- logit_scale: float32 [1], replicated, may hold values from 4 to 16
- logit_bias: float32 [1], replicated, may hold values from -3 to -1
Outputs:
- row_loss: float32 [262144], P(('dp', 'contrast')), parts along dimension 0
- grad_image: bfloat16 [262144, 1152], P(('dp', 'contrast')), parts along dimension 0
- grad_text: bfloat16 [262144, 1152], P(('dp', 'contrast')), parts along dimension 0
There are 32 independent parts, one for each index of `dp`. A program takes and returns all parts, laid end to end along the dimension named above; an argument that names none is the same for every part. Nothing has to cross between parts.
All inputs are finite; a program needn't handle non-finite values.
Results may differ from a plain program's by a relative error of at most 0.006.
Values may be sent and summed in bfloat16 or wider, within the bound.
A program may use at most 64 MiB of HBM per device.

v0:
```python
import jax
import jax.numpy as jnp
from jax import lax
from jax.sharding import PartitionSpec as P


def swapped(value, axis, distance):
    mask = 2**distance
    pairs = [(source, source ^ mask) for source in range(lax.axis_size(axis))]
    return lax.ppermute(value, axis, pairs)


def normalize(emb):
    full = emb.astype(jnp.float32)
    inv = lax.rsqrt(jnp.sum(full * full, axis=1, keepdims=True) + 1e-06)
    unit = full * inv
    return (unit, inv, unit.astype(jnp.bfloat16))


def pair_terms(xn, yn, scale, bias, diagonal):
    raw = lax.dot_general(xn, yn, (((1,), (1,)), ((), ())), preferred_element_type=jnp.float32)
    score = scale * raw + bias
    if diagonal:
        sign = jnp.where(jnp.eye(xn.shape[0], dtype=jnp.bool_), 1.0, -1.0).astype(jnp.float32)
    else:
        sign = -jnp.ones_like(score)
    loss = jnp.sum(jax.nn.softplus(-sign * score), axis=1)
    slope = (-sign * jax.nn.sigmoid(-sign * score)).astype(jnp.bfloat16)
    grad_x = scale * jnp.dot(slope, yn, preferred_element_type=jnp.float32)
    grad_y = scale * lax.dot_general(
        slope, xn, (((0,), (0,)), ((), ())), preferred_element_type=jnp.float32
    )
    return (loss, grad_x, grad_y)


def finish(unit, inv, grad):
    return ((grad - unit * jnp.sum(unit * grad, axis=1, keepdims=True)) * inv).astype(jnp.bfloat16)


def local(image_emb, text_emb, logit_scale, logit_bias):
    scale = logit_scale[0]
    bias = logit_bias[0]
    unit_x, inv_x, xn = normalize(image_emb)
    unit_y, inv_y, yn = normalize(text_emb)
    rows = xn.shape[0]
    total, grad_x, grad_y = pair_terms(xn, yn, scale, bias, True)
    far_bit = lax.axis_size("contrast").bit_length() - 2
    for bit in [far_bit, 0]:
        other_y = swapped(yn, "contrast", bit)
        loss, gx, partner_gy = pair_terms(xn, other_y, scale, bias, False)
        total = total + loss
        grad_x = grad_x + gx
        grad_y = grad_y + swapped(partner_gy, "contrast", bit)
    row_loss = total / (3.0 * rows)
    return (row_loss, finish(unit_x, inv_x, grad_x), finish(unit_y, inv_y, grad_y))


def solution(mesh):
    placed = (P(("dp", "contrast"), None), P(("dp", "contrast"), None), P(), P())
    return jax.shard_map(
        local,
        mesh=mesh,
        in_specs=placed,
        out_specs=(P(("dp", "contrast")), P(("dp", "contrast"), None), P(("dp", "contrast"), None)),
        check_vma=False,
    )
```

profile of v0, /device:TPU:105, one launch (start us, length us, event | category | flops | bytes accessed | tf_op | source)
XLA Modules:
  0.0 177.5 jit_solution(10414569172238896131)
XLA Ops:
  0.6 0.0 copy-start.1
  0.6 1.7 fusion.18
  2.3 1.5 fusion.5
  3.9 3.1 %collective-permute-start.1 = (bf16[512,1152]{1,0:T(8,128)(2,1)S(1)}, bf16[512,1152]{1,0:T(8,128)(2,1)S(1)}, u32[]{:S(2)}, u32[]{:S(2)}) collective-permute-start(bf16[512,1152]{1,0:T(8,128)(2,1)S(1)} %fusion.5), channel_id=1, source_target_pairs={{0,32},{32,0},{64,96},{96,64},{128,160},{160,128},{192,224},{224,1... | collective-permute-start | bytes 3538952 | tf_op jit(solution)/shard_map/ppermute | solution.py:10
  7.0 9.7 %collective-permute-start = (bf16[512,1152]{1,0:T(8,128)(2,1)S(1)}, bf16[512,1152]{1,0:T(8,128)(2,1)S(1)}, u32[]{:S(2)}, u32[]{:S(2)}) collective-permute-start(bf16[512,1152]{1,0:T(8,128)(2,1)S(1)} %fusion.5), channel_id=1, source_target_pairs={{0,256},{32,288},{64,320},{96,352},{128,384},{160,416},{192,448},{... | collective-permute-start | bytes 3538952 | tf_op jit(solution)/shard_map/ppermute | solution.py:10
  18.0 0.0 copy-done.1
  18.0 0.3 fusion.13
  18.4 14.2 %collective-permute-done.1 = bf16[512,1152]{1,0:T(8,128)(2,1)S(1)} collective-permute-done((bf16[512,1152]{1,0:T(8,128)(2,1)S(1)}, bf16[512,1152]{1,0:T(8,128)(2,1)S(1)}, u32[]{:S(2)}, u32[]{:S(2)}) %collective-permute-start.1) | collective-permute-done | bytes 1179680 | tf_op jit(solution)/shard_map/ppermute | solution.py:10
  32.6 1.5 fusion.25
  34.1 1.1 convolution_multiply_fusion
  35.2 3.1 %collective-permute-start.3 = (f32[512,1152]{1,0:T(8,128)S(1)}, f32[512,1152]{1,0:T(8,128)S(1)}, u32[]{:S(2)}, u32[]{:S(2)}) collective-permute-start(f32[512,1152]{1,0:T(8,128)S(1)} %convolution_multiply_fusion), channel_id=1, source_target_pairs={{0,32},{32,0},{64,96},{96,64},{128,160},{160,128},{192,224},{224,1... | collective-permute-start | bytes 7077896 | tf_op jit(solution)/shard_map/ppermute | solution.py:10
  38.3 29.2 %collective-permute-done = bf16[512,1152]{1,0:T(8,128)(2,1)S(1)} collective-permute-done((bf16[512,1152]{1,0:T(8,128)(2,1)S(1)}, bf16[512,1152]{1,0:T(8,128)(2,1)S(1)}, u32[]{:S(2)}, u32[]{:S(2)}) %collective-permute-start) | collective-permute-done | bytes 1179680 | tf_op jit(solution)/shard_map/ppermute | solution.py:10
  67.5 1.5 fusion.24
  69.0 1.1 convolution_multiply_fusion.1
  70.2 6.9 %collective-permute-start.2 = (f32[512,1152]{1,0:T(8,128)S(1)}, f32[512,1152]{1,0:T(8,128)S(1)}, u32[]{:S(2)}, u32[]{:S(2)}) collective-permute-start(f32[512,1152]{1,0:T(8,128)S(1)} %convolution_multiply_fusion.1), channel_id=1, source_target_pairs={{0,256},{32,288},{64,320},{96,352},{128,384},{160,416},{192,448},{... | collective-permute-start | bytes 7077896 | tf_op jit(solution)/shard_map/ppermute | solution.py:10
  77.1 1.6 fusion.23
  78.6 0.9 fusion.26
  79.5 0.6 add_multiply_fusion
  80.1 0.9 convolution_add_fusion.1
  81.1 1.2 fusion.9
  82.3 0.0 copy-start
  82.3 1.5 fusion.12
  83.8 4.5 %collective-permute-done.3 = f32[512,1152]{1,0:T(8,128)S(1)} collective-permute-done((f32[512,1152]{1,0:T(8,128)S(1)}, f32[512,1152]{1,0:T(8,128)S(1)}, u32[]{:S(2)}, u32[]{:S(2)}) %collective-permute-start.3) | collective-permute-done | bytes 2359328 | tf_op jit(solution)/shard_map/ppermute | solution.py:10
  88.3 86.3 %collective-permute-done.2 = f32[512,1152]{1,0:T(8,128)S(1)} collective-permute-done((f32[512,1152]{1,0:T(8,128)S(1)}, f32[512,1152]{1,0:T(8,128)S(1)}, u32[]{:S(2)}, u32[]{:S(2)}) %collective-permute-start.2) | collective-permute-done | bytes 2359328 | tf_op jit(solution)/shard_map/ppermute | solution.py:10
  174.6 0.0 copy-done
  174.6 1.3 fusion.14
  175.9 1.5 fusion.17
  (2 shorter events, 0.0 us)
Async XLA Ops:
  0.6 17.4 %copy-start.1 = (bf16[512,1152]{1,0:T(8,128)(2,1)S(1)}, bf16[512,1152]{1,0:T(8,128)(2,1)}, u32[]{:S(2)}) copy-start(bf16[512,1152]{1,0:T(8,128)(2,1)} %param.4) | copy-start | bytes 3538948
  3.9 28.7 %collective-permute-start.1 = (bf16[512,1152]{1,0:T(8,128)(2,1)S(1)}, bf16[512,1152]{1,0:T(8,128)(2,1)S(1)}, u32[]{:S(2)}, u32[]{:S(2)}) collective-permute-start(bf16[512,1152]{1,0:T(8,128)(2,1)S(1)} %fusion.5), channel_id=1, source_target_pairs={{0,32},{32,0},{64,96},{96,64},{128,160},{160,128},{192,224},{224,1... | collective-permute-start | bytes 3538952 | tf_op jit(solution)/shard_map/ppermute | solution.py:10
  7.0 60.6 %collective-permute-start = (bf16[512,1152]{1,0:T(8,128)(2,1)S(1)}, bf16[512,1152]{1,0:T(8,128)(2,1)S(1)}, u32[]{:S(2)}, u32[]{:S(2)}) collective-permute-start(bf16[512,1152]{1,0:T(8,128)(2,1)S(1)} %fusion.5), channel_id=1, source_target_pairs={{0,256},{32,288},{64,320},{96,352},{128,384},{160,416},{192,448},{... | collective-permute-start | bytes 3538952 | tf_op jit(solution)/shard_map/ppermute | solution.py:10
  35.2 53.1 %collective-permute-start.3 = (f32[512,1152]{1,0:T(8,128)S(1)}, f32[512,1152]{1,0:T(8,128)S(1)}, u32[]{:S(2)}, u32[]{:S(2)}) collective-permute-start(f32[512,1152]{1,0:T(8,128)S(1)} %convolution_multiply_fusion), channel_id=1, source_target_pairs={{0,32},{32,0},{64,96},{96,64},{128,160},{160,128},{192,224},{224,1... | collective-permute-start | bytes 7077896 | tf_op jit(solution)/shard_map/ppermute | solution.py:10
  70.2 104.5 %collective-permute-start.2 = (f32[512,1152]{1,0:T(8,128)S(1)}, f32[512,1152]{1,0:T(8,128)S(1)}, u32[]{:S(2)}, u32[]{:S(2)}) collective-permute-start(f32[512,1152]{1,0:T(8,128)S(1)} %convolution_multiply_fusion.1), channel_id=1, source_target_pairs={{0,256},{32,288},{64,320},{96,352},{128,384},{160,416},{192,448},{... | collective-permute-start | bytes 7077896 | tf_op jit(solution)/shard_map/ppermute | solution.py:10
  82.3 92.3 %copy-start = (bf16[512,1152]{1,0:T(8,128)(2,1)S(1)}, bf16[512,1152]{1,0:T(8,128)(2,1)}, u32[]{:S(2)}) copy-start(bf16[512,1152]{1,0:T(8,128)(2,1)} %param.5) | copy-start | bytes 3538948
where the time goes:
time: 178 us; the launch traced here: 177 us
  waiting for transfers between devices  134 us (75%)
  starting transfers between devices  22.9 us (13%)
  matrix products  11.1 us (6%)
  other arithmetic  7.14 us (4%)
  between operations  2.03 us (1%)
    ppermute x4, waiting for transfers between devices, swapped(): return lax.ppermute(value, axis, pairs)  134 us
    ppermute x4, starting transfers between devices, swapped(): return lax.ppermute(value, axis, pairs)  22.9 us
    dot_general x3, matrix products, pair_terms(): lax.dot_general(xn, yn, (((1,), (1,)), ((), ())), preferred_element_type=...  4.55 us
  transfers between devices with their start and end apart: 4, of which 4 were waited for; matrix products, arithmetic and copies ran while one was open for 7% of the time, Pallas kernels for 0%

commit v1 on v0

v1 whole, which is shorter than its diff:
```python
import functools

import jax
import jax.numpy as jnp
from jax import lax
from jax.experimental import pallas as pl
from jax.experimental.pallas import tpu as pltpu
from jax.sharding import PartitionSpec as P

MESH = pl.DeviceIdType.MESH
PIECE = 64
CHUNK = 128
FINISH = 64


def kernel(
    n,
    scale_ref,
    bias_ref,
    x_hbm,
    y_hbm,
    loss_out,
    gx_out,
    gy_out,
    raw,
    own,
    far,
    near,
    acc,
    inv,
    loss,
    load_sem,
    far_send,
    far_recv,
    near_send,
    near_recv,
    out_sem,
):
    rows, width = x_hbm.shape
    pieces = rows // PIECE
    me = lax.axis_index("contrast")
    far_id = {"contrast": lax.rem(me + n // 2, n)}
    near_id = {"contrast": me + 1 - 2 * lax.rem(me, 2)}
    scale = scale_ref[0]
    bias = bias_ref[0]

    barrier = pltpu.get_barrier_semaphore()
    for partner in (far_id, near_id):
        pl.semaphore_signal(barrier, inc=1, device_id=partner, device_id_type=MESH)

    def load(side, piece):
        source = (y_hbm, x_hbm)[side]
        return pltpu.make_async_copy(
            source.at[pl.ds(pl.multiple_of(piece * PIECE, PIECE), PIECE)],
            raw.at[pl.ds(pl.multiple_of(side * rows + piece * PIECE, PIECE), PIECE)],
            load_sem.at[side * pieces + piece],
        )

    def remote(target, buffer, send_sem, recv_sem, piece):
        at = pl.ds(pl.multiple_of(piece * PIECE, PIECE), PIECE)
        return pltpu.make_async_remote_copy(
            src_ref=own.at[at],
            dst_ref=buffer.at[at],
            send_sem=send_sem.at[piece],
            recv_sem=recv_sem.at[piece],
            device_id=target,
            device_id_type=MESH,
        )

    to_far = functools.partial(remote, far_id, far, far_send, far_recv)
    to_near = functools.partial(remote, near_id, near, near_send, near_recv)

    for side in (0, 1):
        @pl.loop(0, pieces)
        def _(piece):
            load(side, piece).start()

    for side in (0, 1):
        @pl.loop(0, pieces)
        def _(piece):
            load(side, piece).wait()
            at = pl.ds(pl.multiple_of(side * rows + piece * PIECE, PIECE), PIECE)
            full = raw[at, :].astype(jnp.float32)
            scaled = lax.rsqrt(jnp.sum(full * full, axis=1, keepdims=True) + 1e-06)
            inv[at, :] = scaled
            own[at, :] = (full * scaled).astype(jnp.bfloat16)
            if side == 0:
                @pl.when(piece == 0)
                def _():
                    pl.semaphore_wait(barrier, 2)
            to_far(side * pieces + piece).start()
            to_near(side * pieces + piece).start()

    acc[...] = jnp.zeros_like(acc)
    loss[...] = jnp.zeros_like(loss)

    def products(side, source, step, diagonal=False):
        other = (1 - side) * rows
        at = pl.ds(pl.multiple_of(side * rows + step * CHUNK, CHUNK), CHUNK)
        block = source[at, :]
        product = lax.dot_general(
            own[other:other + rows, :], block, (((1,), (1,)), ((), ())), preferred_element_type=jnp.float32
        )
        value = scale * product + bias
        if diagonal:
            row = lax.broadcasted_iota(jnp.int32, value.shape, 0)
            column = lax.broadcasted_iota(jnp.int32, value.shape, 1) + step * CHUNK
            matched = row == column
            value = jnp.where(matched, -value, value)
        small = jnp.exp(-jnp.abs(value))
        slope = jnp.where(value >= 0, 1.0, small) / (1.0 + small)
        if side == 0:
            loss[...] += jnp.maximum(value, 0.0) + jnp.log1p(small)
        if diagonal:
            slope = jnp.where(matched, -slope, slope)
        slope = slope.astype(jnp.bfloat16)
        mine = pl.ds(side * rows, rows)
        for start in range(0, width, 384):
            columns = slice(start, min(start + 384, width))
            acc[mine, columns] += jnp.dot(slope, block[:, columns], preferred_element_type=jnp.float32)

    for side in (0, 1):
        @pl.loop(0, rows // CHUNK)
        def _(step):
            products(side, own, step, diagonal=True)

    def finish(side, target):
        def out(step):
            at = pl.ds(pl.multiple_of(step * FINISH, FINISH), FINISH)
            here = pl.ds(pl.multiple_of((1 - side) * rows + step * FINISH, FINISH), FINISH)
            return here, pltpu.make_async_copy(raw.at[here], target.at[at], out_sem.at[side * (rows // FINISH) + step])

        @pl.loop(0, rows // FINISH)
        def _(step):
            here, copy = out(step)
            grad = scale * acc[pl.ds(pl.multiple_of(side * rows + step * FINISH, FINISH), FINISH), :]
            scaled = inv[here, :]
            unit = raw[here, :].astype(jnp.float32) * scaled
            along = jnp.sum(unit * grad, axis=1, keepdims=True)
            raw[here, :] = ((grad - unit * along) * scaled).astype(jnp.bfloat16)
            copy.start()

        return out

    per = CHUNK // PIECE
    outs = []
    for side, target in ((0, gx_out), (1, gy_out)):
        @pl.loop(0, rows // CHUNK)
        def _(step):
            for part in range(per):
                to_near(side * pieces + step * per + part).wait_recv()
            products(side, near, step)
            for part in range(per):
                to_far(side * pieces + step * per + part).wait_recv()
            products(side, far, step)

        if side == 0:
            loss_out[...] = jnp.sum(loss[...].T, axis=0) / (3.0 * rows)
        outs.append(finish(side, target))

    for out in outs:
        @pl.loop(0, rows // FINISH)
        def _(step):
            out(step)[1].wait()

    @pl.loop(0, 2 * pieces)
    def _(piece):
        to_far(piece).wait_send()
        to_near(piece).wait_send()


def local(image_emb, text_emb, logit_scale, logit_bias):
    rows, width = image_emb.shape
    n = lax.axis_size("contrast")
    copies = 2 * rows // PIECE
    both = pltpu.VMEM((2 * rows, width), jnp.bfloat16)
    dma = pltpu.SemaphoreType.DMA
    return pl.pallas_call(
        functools.partial(kernel, n),
        out_shape=(
            jax.ShapeDtypeStruct((rows,), jnp.float32),
            jax.ShapeDtypeStruct((rows, width), jnp.bfloat16),
            jax.ShapeDtypeStruct((rows, width), jnp.bfloat16),
        ),
        in_specs=[
            pl.BlockSpec(memory_space=pltpu.SMEM),
            pl.BlockSpec(memory_space=pltpu.SMEM),
            pl.BlockSpec(memory_space=pl.ANY),
            pl.BlockSpec(memory_space=pl.ANY),
        ],
        out_specs=(
            pl.BlockSpec(memory_space=pltpu.VMEM),
            pl.BlockSpec(memory_space=pl.ANY),
            pl.BlockSpec(memory_space=pl.ANY),
        ),
        scratch_shapes=[
            both,
            both,
            both,
            both,
            pltpu.VMEM((2 * rows, width), jnp.float32),
            pltpu.VMEM((2 * rows, 1), jnp.float32),
            pltpu.VMEM((rows, CHUNK), jnp.float32),
            dma((copies,)),
            dma((copies,)),
            dma((copies,)),
            dma((copies,)),
            dma((copies,)),
            dma((2 * rows // FINISH,)),
        ],
        compiler_params=pltpu.CompilerParams(
            collective_id=0, has_side_effects=True, vmem_limit_bytes=40 * 2**20
        ),
        cost_estimate=pl.CostEstimate(
            flops=24 * rows * rows * width, bytes_accessed=8 * rows * width, transcendentals=18 * rows * rows
        ),
        name="contrast",
    )(logit_scale, logit_bias, image_emb, text_emb)


def solution(mesh):
    placed = (P(("dp", "contrast"), None), P(("dp", "contrast"), None), P(), P())
    return jax.shard_map(
        local,
        mesh=mesh,
        in_specs=placed,
        out_specs=(P(("dp", "contrast")), P(("dp", "contrast"), None), P(("dp", "contrast"), None)),
        check_vma=False,
    )
```

time: 178 us -> 126 us (0.71)
  the two profiles are of different devices: /device:TPU:105 before, /device:TPU:143 now
where the time goes in v1:
time: 126 us
  Pallas kernels  119 us (94%)
  local copies, waits for them, and re-layouts  5.14 us (4%)
  between operations  1.94 us (2%)
    pallas_call x1, Pallas kernels, local(): pl.pallas_call(functools.partial(kernel, n), out_shape=(jax.ShapeDtypeStr...  119 us
    unnamed x7, local copies, waits for them, and re-layouts  5.14 us

profile of v1, /device:TPU:143, one launch (start us, length us, event | category | flops | bytes accessed | tf_op | source)
XLA Modules:
  0.0 125.6 jit_solution(372261495298423432)
XLA Ops:
  1.9 0.0 copy-start
  1.9 1.3 %copy-done = bf16[512,1152]{1,0:T(8,128)(2,1)S(1)} copy-done((bf16[512,1152]{1,0:T(8,128)(2,1)S(1)}, bf16[512,1152]{1,0:T(8,128)(2,1)}, u32[]{:S(2)}) %copy-start) | copy-done | bytes 1179672
  3.2 0.0 copy-start.1
  3.2 1.3 %copy-done.1 = bf16[512,1152]{1,0:T(8,128)(2,1)S(1)} copy-done((bf16[512,1152]{1,0:T(8,128)(2,1)S(1)}, bf16[512,1152]{1,0:T(8,128)(2,1)}, u32[]{:S(2)}) %copy-start.1) | copy-done | bytes 1179672
  4.5 118.6 %contrast.1 = (f32[512]{0:T(512)S(1)}, bf16[512,1152]{1,0:T(8,128)(2,1)S(1)}, bf16[512,1152]{1,0:T(8,128)(2,1)S(1)}) custom-call(f32[1]{0:T(128)S(6)} %copy.10.scale_ref, f32[1]{0:T(128)S(6)} %copy.11.bias_ref, bf16[512,1152]{1,0:T(8,128)(2,1)S(1)} %copy-done, bf16[512,1152]{1,0:T(8,128)(2,1)S(1)} %copy-done.1), custom_call_target="tpu_custom_call" | custom-call | flops 7247757312 | bytes 4718592 | tf_op jit(solution)/shard_map/contrast/pallas_call | solution.py:178
  123.0 0.6 copy.12
  123.6 1.0 copy.13
  124.6 1.0 copy.14
Async XLA Ops:
  1.9 1.3 %copy-start = (bf16[512,1152]{1,0:T(8,128)(2,1)S(1)}, bf16[512,1152]{1,0:T(8,128)(2,1)}, u32[]{:S(2)}) copy-start(bf16[512,1152]{1,0:T(8,128)(2,1)} %x_hbm.1) | copy-start | bytes 3538948
  3.2 1.3 %copy-start.1 = (bf16[512,1152]{1,0:T(8,128)(2,1)S(1)}, bf16[512,1152]{1,0:T(8,128)(2,1)}, u32[]{:S(2)}) copy-start(bf16[512,1152]{1,0:T(8,128)(2,1)} %y_hbm.1) | copy-start | bytes 3538948

commit v2 on v1

v2 whole, which is shorter than its diff:
```python
import functools

import jax
import jax.numpy as jnp
from jax import lax
from jax.experimental import pallas as pl
from jax.experimental.pallas import tpu as pltpu
from jax.sharding import PartitionSpec as P

MESH = pl.DeviceIdType.MESH
PIECE = 64
CHUNK = 128
FINISH = 64


def block(index, size, base=0):
    return pl.ds(pl.multiple_of(base + index * size, size), size)


def exchange(
    n,
    scale_hbm,
    bias_hbm,
    image_hbm,
    text_hbm,
    loss_out,
    image_grad,
    text_acc,
    text,
    text_inv,
    text_factor,
    image,
    image_inv,
    image_acc,
    own,
    far,
    near,
    loss,
    scale_ref,
    bias_ref,
    scalar_sem,
    load_sem,
    far_send,
    far_recv,
    near_send,
    near_recv,
):
    rows, width = image_hbm.shape
    pieces = rows // PIECE
    me = lax.axis_index("contrast")
    far_id = {"contrast": lax.rem(me + n // 2, n)}
    near_id = {"contrast": me + 1 - 2 * lax.rem(me, 2)}

    barrier = pltpu.get_barrier_semaphore()
    for partner in (far_id, near_id):
        pl.semaphore_signal(barrier, inc=1, device_id=partner, device_id_type=MESH)

    given = (text_hbm, image_hbm)
    held = (text, image)
    inverse = (text_inv, image_inv)
    total = (image_acc, text_acc)

    def load(side, piece):
        at = block(piece, PIECE)
        return pltpu.make_async_copy(given[side].at[at], held[side].at[at], load_sem.at[side * pieces + piece])

    def remote(target, buffer, send_sem, recv_sem, piece):
        at = block(piece, PIECE)
        return pltpu.make_async_remote_copy(
            src_ref=own.at[at],
            dst_ref=buffer.at[at],
            send_sem=send_sem.at[piece],
            recv_sem=recv_sem.at[piece],
            device_id=target,
            device_id_type=MESH,
        )

    to_far = functools.partial(remote, far_id, far, far_send, far_recv)
    to_near = functools.partial(remote, near_id, near, near_send, near_recv)

    load(0, 0).start()
    scalars = [
        pltpu.make_async_copy(source, target, scalar_sem.at[i])
        for i, (source, target) in enumerate(((scale_hbm, scale_ref), (bias_hbm, bias_ref)))
    ]
    for copy in scalars:
        copy.start()

    @pl.loop(1, pieces)
    def _(piece):
        load(0, piece).start()

    @pl.loop(0, pieces)
    def _(piece):
        load(1, piece).start()

    def prepare(side, piece):
        load(side, piece).wait()
        at = block(piece, PIECE)
        full = held[side][at, :].astype(jnp.float32)
        scaled = lax.rsqrt(jnp.sum(full * full, axis=1, keepdims=True) + 1e-06)
        inverse[side][at, :] = scaled
        own[block(piece, PIECE, side * rows), :] = (full * scaled).astype(jnp.bfloat16)

    def send(side, piece):
        to_far(side * pieces + piece).start()
        to_near(side * pieces + piece).start()

    prepare(0, 0)
    pl.semaphore_wait(barrier, 2)
    send(0, 0)
    for side in (0, 1):
        @pl.loop(1 - side, pieces)
        def _(piece):
            prepare(side, piece)
            send(side, piece)

    for copy in scalars:
        copy.wait()
    scale = scale_ref[0, 0]
    bias = bias_ref[0, 0]
    text_factor[...] = scale * text_inv[...]
    image_acc[...] = jnp.zeros_like(image_acc)
    text_acc[...] = jnp.zeros_like(text_acc)
    loss[...] = jnp.zeros_like(loss)

    def products(side, source, step, diagonal=False):
        other = (1 - side) * rows
        here = source[block(step, CHUNK, side * rows), :]
        product = lax.dot_general(
            own[other:other + rows, :], here, (((1,), (1,)), ((), ())), preferred_element_type=jnp.float32
        )
        value = scale * product + bias
        if diagonal:
            row = lax.broadcasted_iota(jnp.int32, value.shape, 0)
            column = lax.broadcasted_iota(jnp.int32, value.shape, 1) + step * CHUNK
            matched = row == column
            value = jnp.where(matched, -value, value)
        small = jnp.exp(-jnp.abs(value))
        slope = jnp.where(value >= 0, 1.0, small) / (1.0 + small)
        if side == 0:
            loss[...] += jnp.maximum(value, 0.0) + jnp.log1p(small)
        if diagonal:
            slope = jnp.where(matched, -slope, slope)
        slope = slope.astype(jnp.bfloat16)
        for start in range(0, width, 384):
            columns = slice(start, min(start + 384, width))
            total[side][:, columns] += jnp.dot(slope, here[:, columns], preferred_element_type=jnp.float32)

    for side in (0, 1):
        @pl.loop(0, rows // CHUNK)
        def _(step):
            products(side, own, step, diagonal=True)

    per = CHUNK // PIECE
    steps = rows // CHUNK

    def arrived(copy, side, step):
        for part in range(per):
            copy(side * pieces + step * per + part).wait_recv()

    def sent(copy, start, stop):
        @pl.loop(start, stop)
        def _(piece):
            copy(piece).wait_send()

    for side in (0, 1):
        @pl.loop(0, steps - side)
        def _(step):
            arrived(to_near, side, step)
            products(side, near, step)
            arrived(to_far, side, step)
            products(side, far, step)

        if side == 0:
            loss_out[...] = jnp.sum(loss[...].T, axis=0) / (3.0 * rows)
            @pl.loop(0, rows // FINISH)
            def _(step):
                at = block(step, FINISH)
                finish(at, image, image_inv, scale * image_inv[at, :], image_acc, image_grad)

    arrived(to_near, 1, steps - 1)
    products(1, near, steps - 1)
    sent(to_far, 0, pieces)
    sent(to_near, 0, 2 * pieces)
    arrived(to_far, 1, steps - 1)
    products(1, far, steps - 1)
    sent(to_far, pieces, 2 * pieces)


def finish(at, emb, inverse, factor, acc, out):
    grad = acc[at, :]
    unit = emb[at, :].astype(jnp.float32) * inverse[at, :]
    along = jnp.sum(unit * grad, axis=1, keepdims=True)
    out[at, :] = ((grad - unit * along) * factor).astype(jnp.bfloat16)


def write(loss, image_grad, text_acc, text, text_inv, text_factor, loss_out, image_out, text_out, text_grad, sem):
    rows = text.shape[0]
    steps = rows // FINISH
    early = [pltpu.make_async_copy(image_grad, image_out, sem.at[steps]), pltpu.make_async_copy(loss, loss_out, sem.at[steps + 1])]
    for copy in early:
        copy.start()
    late = []
    for step in range(steps):
        at = slice(step * FINISH, (step + 1) * FINISH)
        finish(at, text, text_inv, text_factor[at, :], text_acc, text_grad)
        late.append(pltpu.make_async_copy(text_grad.at[at], text_out.at[at], sem.at[step]))
        late[-1].start()
    for copy in early + late:
        copy.wait()


def local(image_emb, text_emb, logit_scale, logit_bias):
    rows, width = image_emb.shape
    n = lax.axis_size("contrast")
    copies = 2 * rows // PIECE
    both = pltpu.VMEM((2 * rows, width), jnp.bfloat16)
    dma = pltpu.SemaphoreType.DMA
    shape = jax.ShapeDtypeStruct
    vmem = pl.BlockSpec(memory_space=pltpu.VMEM)
    hbm = pl.BlockSpec(memory_space=pltpu.HBM)
    handed = pl.pallas_call(
        functools.partial(exchange, n),
        out_shape=(
            shape((rows,), jnp.float32),
            shape((rows, width), jnp.bfloat16),
            shape((rows, width), jnp.float32),
            shape((rows, width), jnp.bfloat16),
            shape((rows, 1), jnp.float32),
            shape((rows, 1), jnp.float32),
        ),
        in_specs=[hbm] * 4,
        out_specs=(vmem,) * 6,
        scratch_shapes=[
            pltpu.VMEM((rows, width), jnp.bfloat16),
            pltpu.VMEM((rows, 1), jnp.float32),
            pltpu.VMEM((rows, width), jnp.float32),
            both,
            both,
            both,
            pltpu.VMEM((rows, CHUNK), jnp.float32),
            pltpu.SMEM((1, 1), jnp.float32),
            pltpu.SMEM((1, 1), jnp.float32),
            dma((2,)),
            dma((copies,)),
            dma((copies,)),
            dma((copies,)),
            dma((copies,)),
            dma((copies,)),
        ],
        compiler_params=pltpu.CompilerParams(
            collective_id=0, has_side_effects=True, vmem_limit_bytes=32 * 2**20
        ),
        cost_estimate=pl.CostEstimate(
            flops=24 * rows * rows * width, bytes_accessed=8 * rows * width, transcendentals=18 * rows * rows
        ),
        name="exchange",
    )(
        logit_scale.reshape(1, 1),
        logit_bias.reshape(1, 1),
        pltpu.with_memory_space_constraint(image_emb, pltpu.HBM),
        pltpu.with_memory_space_constraint(text_emb, pltpu.HBM),
    )
    return pl.pallas_call(
        write,
        out_shape=(
            shape((rows,), jnp.float32),
            shape((rows, width), jnp.bfloat16),
            shape((rows, width), jnp.bfloat16),
        ),
        in_specs=[vmem] * 6,
        out_specs=(hbm,) * 3,
        scratch_shapes=[pltpu.VMEM((rows, width), jnp.bfloat16), dma((rows // FINISH + 2,))],
        compiler_params=pltpu.CompilerParams(vmem_limit_bytes=16 * 2**20),
        cost_estimate=pl.CostEstimate(flops=8 * rows * width, bytes_accessed=12 * rows * width, transcendentals=0),
        name="write",
    )(*handed)


def solution(mesh):
    placed = (P(("dp", "contrast"), None), P(("dp", "contrast"), None), P(), P())
    return jax.shard_map(
        local,
        mesh=mesh,
        in_specs=placed,
        out_specs=(P(("dp", "contrast")), P(("dp", "contrast"), None), P(("dp", "contrast"), None)),
        check_vma=False,
    )
```

time: 126 us -> 117 us (0.929)
  the two profiles are of different devices: /device:TPU:143 before, /device:TPU:145 now
where the time goes in v2:
time: 117 us
  Pallas kernels  115 us (98%)
  between operations  1.93 us (2%)
    pallas_call x1, Pallas kernels, local(): pl.pallas_call(functools.partial(exchange, n), out_shape=(shape((rows,),...  113 us

profile of v2, /device:TPU:145, one launch (start us, length us, event | category | flops | bytes accessed | tf_op | source)
XLA Modules:
  0.0 117.3 jit_solution(4430598929050984404)
XLA Ops:
  1.9 113.1 %exchange.1 = (f32[512]{0:T(512)S(1)}, bf16[512,1152]{1,0:T(8,128)(2,1)S(1)}, f32[512,1152]{1,0:T(8,128)S(1)}, bf16[512,1152]{1,0:T(8,128)(2,1)S(1)}, f32[512,1]{1,0:T(8,128)S(1)}, /*index=5*/f32[512,1]{1,0:T(8,128)S(1)}) custom-call(f32[1,1]{1,0:T(1,128)} %bitcast.2.scale_hbm, f32[1,1]{1,0:T(1,128)} %bitcast.3.bias_hbm, bf16[512,1152]{1,0:T(8,128)(2,1)} %image_hbm.1, ...), custom_call_target="tpu_custom_call" | custom-call | flops 7247757312 | bytes 4718592 | tf_op jit(solution)/shard_map/exchange/pallas_call | solution.py:223
  115.1 2.2 %write.1 = (f32[512]{0:T(512)}, bf16[512,1152]{1,0:T(8,128)(2,1)}, bf16[512,1152]{1,0:T(8,128)(2,1)}) custom-call(f32[512]{0:T(512)S(1)} %get-tuple-element.9.loss, bf16[512,1152]{1,0:T(8,128)(2,1)S(1)} %get-tuple-element.10.image_grad, f32[512,1152]{1,0:T(8,128)S(1)} %get-tuple-element.11.text_acc, bf16[512,1152]{1,0:T(8,128)(2,1)S(1)} %get-tuple-element.12.text, ...), custom_call_target="tpu_custom_call" | custom-call | flops 4718592 | bytes 7077888 | tf_op jit(solution)/shard_map/write/pallas_call | solution.py:265

commit v3 on v2

v3 whole, which is shorter than its diff:
```python
import functools

import jax
import jax.numpy as jnp
from jax import lax
from jax.experimental import pallas as pl
from jax.experimental.pallas import tpu as pltpu
from jax.sharding import PartitionSpec as P

MESH = pl.DeviceIdType.MESH
PIECE = 64
CHUNK = 128
FINISH = 64
WRITE = 128


def block(index, size, base=0):
    return pl.ds(pl.multiple_of(base + index * size, size), size)


def exchange(
    n,
    scale_hbm,
    bias_hbm,
    image_hbm,
    text_hbm,
    loss_out,
    image_grad,
    text_grad,
    text,
    text_inv,
    text_acc,
    image,
    image_inv,
    image_acc,
    own,
    far,
    near,
    back,
    loss,
    scale_ref,
    bias_ref,
    scalar_sem,
    load_sem,
    far_send,
    far_recv,
    near_send,
    near_recv,
):
    rows, width = image_hbm.shape
    pieces = rows // PIECE
    me = lax.axis_index("contrast")
    far_id = {"contrast": lax.rem(me + n // 2, n)}
    near_id = {"contrast": me + 1 - 2 * lax.rem(me, 2)}

    barrier = pltpu.get_barrier_semaphore()
    for partner in (far_id, near_id):
        pl.semaphore_signal(barrier, inc=1, device_id=partner, device_id_type=MESH)

    given = (text_hbm, image_hbm)
    held = (text, image)
    inverse = (text_inv, image_inv)
    total = (image_acc, text_acc)

    def load(side, piece):
        at = block(piece, PIECE)
        return pltpu.make_async_copy(given[side].at[at], held[side].at[at], load_sem.at[side * pieces + piece])

    def remote(target, source, at, buffer, to, send_sem, recv_sem, piece):
        return pltpu.make_async_remote_copy(
            src_ref=source.at[at],
            dst_ref=buffer.at[to],
            send_sem=send_sem.at[piece],
            recv_sem=recv_sem.at[piece],
            device_id=target,
            device_id_type=MESH,
        )

    def to_near(piece):
        at = block(piece, PIECE)
        return remote(near_id, own, at, near, at, near_send, near_recv, piece)

    def to_far(piece):
        at = block(piece, PIECE)
        return remote(far_id, own, at, far, at, far_send, far_recv, piece)

    def go_back(piece):
        at = block(piece, PIECE)
        return remote(far_id, back, at, far, block(piece, PIECE, rows), far_send, far_recv, pieces + piece)

    load(0, 0).start()
    scalars = [
        pltpu.make_async_copy(source, target, scalar_sem.at[i])
        for i, (source, target) in enumerate(((scale_hbm, scale_ref), (bias_hbm, bias_ref)))
    ]
    for copy in scalars:
        copy.start()

    @pl.loop(1, pieces)
    def _(piece):
        load(0, piece).start()

    @pl.loop(0, pieces)
    def _(piece):
        load(1, piece).start()

    def prepare(side, piece):
        load(side, piece).wait()
        at = block(piece, PIECE)
        full = held[side][at, :].astype(jnp.float32)
        scaled = lax.rsqrt(jnp.sum(full * full, axis=1, keepdims=True) + 1e-06)
        inverse[side][at, :] = scaled
        own[block(piece, PIECE, side * rows), :] = (full * scaled).astype(jnp.bfloat16)

    prepare(0, 0)
    pl.semaphore_wait(barrier, 2)
    to_far(0).start()
    to_near(0).start()

    @pl.loop(1, pieces)
    def _(piece):
        prepare(0, piece)
        to_far(piece).start()
        to_near(piece).start()

    @pl.loop(0, pieces)
    def _(piece):
        prepare(1, piece)
        to_near(pieces + piece).start()

    for copy in scalars:
        copy.wait()
    scale = scale_ref[0, 0]
    bias = bias_ref[0, 0]
    image_acc[...] = jnp.zeros_like(image_acc)
    text_acc[...] = jnp.zeros_like(text_acc)
    loss[...] = jnp.zeros_like(loss)

    def products(side, source, step, diagonal=False, returned=False):
        other = (1 - side) * rows
        here = source[block(step, CHUNK, side * rows), :]
        product = lax.dot_general(
            own[other:other + rows, :], here, (((1,), (1,)), ((), ())), preferred_element_type=jnp.float32
        )
        value = scale * product + bias
        if diagonal:
            row = lax.broadcasted_iota(jnp.int32, value.shape, 0)
            column = lax.broadcasted_iota(jnp.int32, value.shape, 1) + step * CHUNK
            matched = row == column
            value = jnp.where(matched, -value, value)
        small = jnp.exp(-jnp.abs(value))
        slope = jnp.where(value >= 0, 1.0, small) / (1.0 + small)
        if side == 0:
            loss[...] += jnp.maximum(value, 0.0) + jnp.log1p(small)
        if diagonal:
            slope = jnp.where(matched, -slope, slope)
        slope = slope.astype(jnp.bfloat16)
        for start in range(0, width, 384):
            columns = slice(start, min(start + 384, width))
            total[side][:, columns] += jnp.dot(slope, here[:, columns], preferred_element_type=jnp.float32)
            if returned:
                back[block(step, CHUNK), columns] = lax.dot_general(
                    slope,
                    own[other:other + rows, columns],
                    (((0,), (0,)), ((), ())),
                    preferred_element_type=jnp.float32,
                ).astype(jnp.bfloat16)

    for side in (0, 1):
        @pl.loop(0, rows // CHUNK)
        def _(step):
            products(side, own, step, diagonal=True)

    per = CHUNK // PIECE

    @pl.loop(0, rows // CHUNK)
    def _(step):
        for part in range(per):
            to_far(step * per + part).wait_recv()
        products(0, far, step, returned=True)
        for part in range(per):
            go_back(step * per + part).start()
        for part in range(per):
            to_near(step * per + part).wait_recv()
        products(0, near, step)

    loss_out[...] = jnp.sum(loss[...].T, axis=0) / (3.0 * rows)

    @pl.loop(0, rows // FINISH)
    def _(step):
        at = block(step, FINISH)
        finish(image_acc[at, :], image[at, :], image_inv[at, :], scale, image_grad, at)

    @pl.loop(0, rows // CHUNK)
    def _(step):
        for part in range(per):
            to_near(pieces + step * per + part).wait_recv()
        products(1, near, step)

    @pl.loop(0, pieces)
    def _(piece):
        to_far(piece).wait_send()
        to_near(piece).wait_send()
        to_near(pieces + piece).wait_send()

    @pl.loop(0, pieces)
    def _(piece):
        go_back(piece).wait_recv()
        at = block(piece, PIECE)
        grad = text_acc[at, :] + far[block(piece, PIECE, rows), :].astype(jnp.float32)
        finish(grad, text[at, :], text_inv[at, :], scale, text_grad, at)

    @pl.loop(0, pieces)
    def _(piece):
        go_back(piece).wait_send()


def finish(grad, emb, inverse, scale, out, at):
    unit = emb.astype(jnp.float32) * inverse
    along = jnp.sum(unit * grad, axis=1, keepdims=True)
    out[at, :] = ((grad - unit * along) * (scale * inverse)).astype(jnp.bfloat16)


def write(loss, image_grad, text_grad, loss_out, image_out, text_out, sem):
    rows = image_grad.shape[0]
    copies = [pltpu.make_async_copy(loss, loss_out, sem.at[0])]
    for side, (source, target) in enumerate(((image_grad, image_out), (text_grad, text_out))):
        for step in range(rows // WRITE):
            at = pl.ds(step * WRITE, WRITE)
            copies.append(pltpu.make_async_copy(source.at[at], target.at[at], sem.at[len(copies)]))
    for copy in copies:
        copy.start()
    for copy in copies:
        copy.wait()


def local(image_emb, text_emb, logit_scale, logit_bias):
    rows, width = image_emb.shape
    n = lax.axis_size("contrast")
    copies = 2 * rows // PIECE
    both = pltpu.VMEM((2 * rows, width), jnp.bfloat16)
    dma = pltpu.SemaphoreType.DMA
    shape = jax.ShapeDtypeStruct
    vmem = pl.BlockSpec(memory_space=pltpu.VMEM)
    hbm = pl.BlockSpec(memory_space=pltpu.HBM)
    outs = (shape((rows,), jnp.float32), shape((rows, width), jnp.bfloat16), shape((rows, width), jnp.bfloat16))
    one = pltpu.VMEM((rows, width), jnp.bfloat16)
    wide = pltpu.VMEM((rows, width), jnp.float32)
    column = pltpu.VMEM((rows, 1), jnp.float32)
    handed = pl.pallas_call(
        functools.partial(exchange, n),
        out_shape=outs,
        in_specs=[hbm] * 4,
        out_specs=(vmem,) * 3,
        scratch_shapes=[
            one,
            column,
            wide,
            one,
            column,
            wide,
            both,
            both,
            both,
            one,
            pltpu.VMEM((rows, CHUNK), jnp.float32),
            pltpu.SMEM((1, 1), jnp.float32),
            pltpu.SMEM((1, 1), jnp.float32),
            dma((2,)),
            dma((copies,)),
            dma((copies,)),
            dma((copies,)),
            dma((copies,)),
            dma((copies,)),
        ],
        compiler_params=pltpu.CompilerParams(
            collective_id=0, has_side_effects=True, vmem_limit_bytes=32 * 2**20
        ),
        cost_estimate=pl.CostEstimate(
            flops=22 * rows * rows * width, bytes_accessed=8 * rows * width, transcendentals=15 * rows * rows
        ),
        name="exchange",
    )(
        logit_scale.reshape(1, 1),
        logit_bias.reshape(1, 1),
        pltpu.with_memory_space_constraint(image_emb, pltpu.HBM),
        pltpu.with_memory_space_constraint(text_emb, pltpu.HBM),
    )
    return pl.pallas_call(
        write,
        out_shape=outs,
        in_specs=[vmem] * 3,
        out_specs=(hbm,) * 3,
        scratch_shapes=[dma((2 * rows // WRITE + 1,))],
        compiler_params=pltpu.CompilerParams(vmem_limit_bytes=4 * 2**20),
        cost_estimate=pl.CostEstimate(flops=0, bytes_accessed=8 * rows * width, transcendentals=0),
        name="write",
    )(*handed)


def solution(mesh):
    placed = (P(("dp", "contrast"), None), P(("dp", "contrast"), None), P(), P())
    return jax.shard_map(
        local,
        mesh=mesh,
        in_specs=placed,
        out_specs=(P(("dp", "contrast")), P(("dp", "contrast"), None), P(("dp", "contrast"), None)),
        check_vma=False,
    )
```

time: 117 us -> 116 us (level)
  the two profiles are of different devices: /device:TPU:145 before, /device:TPU:185 now
where the time goes in v3:
time: 116 us; the launch traced here: 115 us
  Pallas kernels  114 us (98%)
  between operations  1.93 us (2%)
    pallas_call x1, Pallas kernels, local(): pl.pallas_call(functools.partial(exchange, n), out_shape=outs, in_specs=[...  112 us

profile of v3, /device:TPU:185, one launch (start us, length us, event | category | flops | bytes accessed | tf_op | source)
XLA Modules:
  0.0 115.5 jit_solution(9552111663144201905)
XLA Ops:
  1.9 112.1 %exchange.1 = (f32[512]{0:T(512)S(1)}, bf16[512,1152]{1,0:T(8,128)(2,1)S(1)}, bf16[512,1152]{1,0:T(8,128)(2,1)S(1)}) custom-call(f32[1,1]{1,0:T(1,128)} %bitcast.2.scale_hbm, f32[1,1]{1,0:T(1,128)} %bitcast.3.bias_hbm, bf16[512,1152]{1,0:T(8,128)(2,1)} %image_hbm.1, bf16[512,1152]{1,0:T(8,128)(2,1)} %text_hbm.1), custom_call_target="tpu_custom_call" | custom-call | flops 6643777536 | bytes 4718592 | tf_op jit(solution)/shard_map/exchange/pallas_call | solution.py:250
  114.0 1.5 %write.1 = (f32[512]{0:T(512)}, bf16[512,1152]{1,0:T(8,128)(2,1)}, bf16[512,1152]{1,0:T(8,128)(2,1)}) custom-call(f32[512]{0:T(512)S(1)} %get-tuple-element.6.loss, bf16[512,1152]{1,0:T(8,128)(2,1)S(1)} %get-tuple-element.7.image_grad, bf16[512,1152]{1,0:T(8,128)(2,1)S(1)} %get-tuple-element.8.text_grad), custom_call_target="tpu_custom_call" | custom-call | bytes 4718592 | tf_op jit(solution)/shard_map/write/pallas_call | solution.py:289

commit v4 on v3

--- a/solution.py
+++ b/solution.py
@@ -8,7 +8,9 @@
 from jax.sharding import PartitionSpec as P
 
 MESH = pl.DeviceIdType.MESH
-PIECE = 64
+PIECE = 128
+TEXT = 128
+PREPARE = 64
 CHUNK = 128
 FINISH = 64
 WRITE = 128
@@ -49,6 +51,8 @@
 ):
     rows, width = image_hbm.shape
     pieces = rows // PIECE
+    sends = rows // TEXT
+    parts = rows // PREPARE
     me = lax.axis_index("contrast")
     far_id = {"contrast": lax.rem(me + n // 2, n)}
     near_id = {"contrast": me + 1 - 2 * lax.rem(me, 2)}
@@ -61,10 +65,6 @@
     held = (text, image)
     inverse = (text_inv, image_inv)
     total = (image_acc, text_acc)
-
-    def load(side, piece):
-        at = block(piece, PIECE)
-        return pltpu.make_async_copy(given[side].at[at], held[side].at[at], load_sem.at[side * pieces + piece])
 
     def remote(target, source, at, buffer, to, send_sem, recv_sem, piece):
         return pltpu.make_async_remote_copy(
@@ -77,18 +77,26 @@
         )
 
     def to_near(piece):
-        at = block(piece, PIECE)
+        at = block(piece, TEXT)
         return remote(near_id, own, at, near, at, near_send, near_recv, piece)
 
     def to_far(piece):
-        at = block(piece, PIECE)
-        return remote(far_id, own, at, far, at, far_send, far_recv, piece)
+        at = block(piece, TEXT)
+        return remote(far_id, text_hbm, at, far, at, far_send, far_recv, piece)
 
     def go_back(piece):
         at = block(piece, PIECE)
-        return remote(far_id, back, at, far, block(piece, PIECE, rows), far_send, far_recv, pieces + piece)
-
-    load(0, 0).start()
+        return remote(far_id, back, at, far, block(piece, PIECE, rows), far_send, far_recv, sends + piece)
+
+    def load(side, piece):
+        at = block(piece, PREPARE)
+        return pltpu.make_async_copy(given[side].at[at], held[side].at[at], load_sem.at[side * parts + piece])
+
+    for side in (0, 1):
+        @pl.loop(0, parts)
+        def _(piece):
+            load(side, piece).start()
+
     scalars = [
         pltpu.make_async_copy(source, target, scalar_sem.at[i])
         for i, (source, target) in enumerate(((scale_hbm, scale_ref), (bias_hbm, bias_ref)))
@@ -96,37 +104,36 @@
     for copy in scalars:
         copy.start()
 
-    @pl.loop(1, pieces)
-    def _(piece):
-        load(0, piece).start()
-
-    @pl.loop(0, pieces)
-    def _(piece):
-        load(1, piece).start()
+    pl.semaphore_wait(barrier, 2)
+
+    @pl.loop(0, sends)
+    def _(piece):
+        to_far(piece).start()
 
     def prepare(side, piece):
         load(side, piece).wait()
-        at = block(piece, PIECE)
-        full = held[side][at, :].astype(jnp.float32)
-        scaled = lax.rsqrt(jnp.sum(full * full, axis=1, keepdims=True) + 1e-06)
+        at = block(piece, PREPARE)
+        unit, scaled = normalize(held[side][at, :])
         inverse[side][at, :] = scaled
-        own[block(piece, PIECE, side * rows), :] = (full * scaled).astype(jnp.bfloat16)
-
-    prepare(0, 0)
-    pl.semaphore_wait(barrier, 2)
-    to_far(0).start()
-    to_near(0).start()
-
-    @pl.loop(1, pieces)
-    def _(piece):
-        prepare(0, piece)
-        to_far(piece).start()
+        own[block(piece, PREPARE, side * rows), :] = unit
+
+    per_send = TEXT // PREPARE
+
+    @pl.loop(0, sends)
+    def _(piece):
+        @pl.loop(0, per_send)
+        def _(part):
+            prepare(0, piece * per_send + part)
+
         to_near(piece).start()
 
-    @pl.loop(0, pieces)
-    def _(piece):
-        prepare(1, piece)
-        to_near(pieces + piece).start()
+    @pl.loop(0, sends)
+    def _(piece):
+        @pl.loop(0, per_send)
+        def _(part):
+            prepare(1, piece * per_send + part)
+
+        to_near(sends + piece).start()
 
     for copy in scalars:
         copy.wait()
@@ -139,6 +146,8 @@
     def products(side, source, step, diagonal=False, returned=False):
         other = (1 - side) * rows
         here = source[block(step, CHUNK, side * rows), :]
+        if returned:
+            here, _ = normalize(here)
         product = lax.dot_general(
             own[other:other + rows, :], here, (((1,), (1,)), ((), ())), preferred_element_type=jnp.float32
         )
@@ -172,17 +181,23 @@
             products(side, own, step, diagonal=True)
 
     per = CHUNK // PIECE
-
-    @pl.loop(0, rows // CHUNK)
-    def _(step):
-        for part in range(per):
-            to_far(step * per + part).wait_recv()
-        products(0, far, step, returned=True)
-        for part in range(per):
-            go_back(step * per + part).start()
-        for part in range(per):
-            to_near(step * per + part).wait_recv()
-        products(0, near, step)
+    steps = TEXT // CHUNK
+
+    @pl.loop(0, sends)
+    def _(piece):
+        to_far(piece).wait_recv()
+
+        @pl.loop(piece * steps, (piece + 1) * steps)
+        def _(step):
+            products(0, far, step, returned=True)
+            for part in range(per):
+                go_back(step * per + part).start()
+
+        to_near(piece).wait_recv()
+
+        @pl.loop(piece * steps, (piece + 1) * steps)
+        def _(step):
+            products(0, near, step)
 
     loss_out[...] = jnp.sum(loss[...].T, axis=0) / (3.0 * rows)
 
@@ -191,17 +206,19 @@
         at = block(step, FINISH)
         finish(image_acc[at, :], image[at, :], image_inv[at, :], scale, image_grad, at)
 
-    @pl.loop(0, rows // CHUNK)
-    def _(step):
-        for part in range(per):
-            to_near(pieces + step * per + part).wait_recv()
-        products(1, near, step)
-
-    @pl.loop(0, pieces)
+    @pl.loop(0, sends)
+    def _(piece):
+        to_near(sends + piece).wait_recv()
+
+        @pl.loop(piece * steps, (piece + 1) * steps)
+        def _(step):
+            products(1, near, step)
+
+    @pl.loop(0, sends)
     def _(piece):
         to_far(piece).wait_send()
         to_near(piece).wait_send()
-        to_near(pieces + piece).wait_send()
+        to_near(sends + piece).wait_send()
 
     @pl.loop(0, pieces)
     def _(piece):
@@ -213,6 +230,12 @@
     @pl.loop(0, pieces)
     def _(piece):
         go_back(piece).wait_send()
+
+
+def normalize(emb):
+    full = emb.astype(jnp.float32)
+    scaled = lax.rsqrt(jnp.sum(full * full, axis=1, keepdims=True) + 1e-06)
+    return (full * scaled).astype(jnp.bfloat16), scaled
 
 
 def finish(grad, emb, inverse, scale, out, at):
@@ -237,7 +260,8 @@
 def local(image_emb, text_emb, logit_scale, logit_bias):
     rows, width = image_emb.shape
     n = lax.axis_size("contrast")
-    copies = 2 * rows // PIECE
+    sends = rows // TEXT
+    copies = sends + rows // PIECE
     both = pltpu.VMEM((2 * rows, width), jnp.bfloat16)
     dma = pltpu.SemaphoreType.DMA
     shape = jax.ShapeDtypeStruct
@@ -267,11 +291,11 @@
             pltpu.SMEM((1, 1), jnp.float32),
             pltpu.SMEM((1, 1), jnp.float32),
             dma((2,)),
+            dma((2 * rows // PREPARE,)),
             dma((copies,)),
             dma((copies,)),
-            dma((copies,)),
-            dma((copies,)),
-            dma((copies,)),
+            dma((2 * sends,)),
+            dma((2 * sends,)),
         ],
         compiler_params=pltpu.CompilerParams(
             collective_id=0, has_side_effects=True, vmem_limit_bytes=32 * 2**20

time: 116 us -> 116 us (level)
  the two profiles are of different devices: /device:TPU:185 before, /device:TPU:122 now
where the time goes in v4:
time: 116 us
  Pallas kernels  114 us (98%)
  between operations  1.93 us (2%)
    pallas_call x1, Pallas kernels, local(): pl.pallas_call(functools.partial(exchange, n), out_shape=outs, in_specs=[...  112 us

profile of v4, /device:TPU:122, one launch (start us, length us, event | category | flops | bytes accessed | tf_op | source)
XLA Modules:
  0.0 115.9 jit_solution(3389667058545330576)
XLA Ops:
  1.9 112.5 %exchange.1 = (f32[512]{0:T(512)S(1)}, bf16[512,1152]{1,0:T(8,128)(2,1)S(1)}, bf16[512,1152]{1,0:T(8,128)(2,1)S(1)}) custom-call(f32[1,1]{1,0:T(1,128)} %bitcast.2.scale_hbm, f32[1,1]{1,0:T(1,128)} %bitcast.3.bias_hbm, bf16[512,1152]{1,0:T(8,128)(2,1)} %image_hbm.1, bf16[512,1152]{1,0:T(8,128)(2,1)} %text_hbm.1), custom_call_target="tpu_custom_call" | custom-call | flops 6643777536 | bytes 4718592 | tf_op jit(solution)/shard_map/exchange/pallas_call | solution.py:274
  114.4 1.5 %write.1 = (f32[512]{0:T(512)}, bf16[512,1152]{1,0:T(8,128)(2,1)}, bf16[512,1152]{1,0:T(8,128)(2,1)}) custom-call(f32[512]{0:T(512)S(1)} %get-tuple-element.6.loss, bf16[512,1152]{1,0:T(8,128)(2,1)S(1)} %get-tuple-element.7.image_grad, bf16[512,1152]{1,0:T(8,128)(2,1)S(1)} %get-tuple-element.8.text_grad), custom_call_target="tpu_custom_call" | custom-call | bytes 4718592 | tf_op jit(solution)/shard_map/write/pallas_call | solution.py:313

commit v5 on v4

--- a/solution.py
+++ b/solution.py
@@ -13,7 +13,7 @@
 PREPARE = 64
 CHUNK = 128
 FINISH = 64
-WRITE = 128
+WRITE = 256
 
 
 def block(index, size, base=0):
@@ -88,6 +88,12 @@
         at = block(piece, PIECE)
         return remote(far_id, back, at, far, block(piece, PIECE, rows), far_send, far_recv, sends + piece)
 
+    pl.semaphore_wait(barrier, 2)
+
+    @pl.loop(0, sends)
+    def _(piece):
+        to_far(piece).start()
+
     def load(side, piece):
         at = block(piece, PREPARE)
         return pltpu.make_async_copy(given[side].at[at], held[side].at[at], load_sem.at[side * parts + piece])
@@ -103,12 +109,6 @@
     ]
     for copy in scalars:
         copy.start()
-
-    pl.semaphore_wait(barrier, 2)
-
-    @pl.loop(0, sends)
-    def _(piece):
-        to_far(piece).start()
 
     def prepare(side, piece):
         load(side, piece).wait()

time: 116 us -> 116 us (level)
  no operation moved by 1% of the time
where the time goes in v5:
time: 116 us
  Pallas kernels  114 us (98%)
  between operations  1.93 us (2%)
    pallas_call x1, Pallas kernels, local(): pl.pallas_call(functools.partial(exchange, n), out_shape=outs, in_specs=[...  112 us

profile of v5, /device:TPU:122, one launch (start us, length us, event | category | flops | bytes accessed | tf_op | source)
XLA Modules:
  0.0 115.8 jit_solution(4679140680938094843)
XLA Ops:
  1.9 112.5 %exchange.1 = (f32[512]{0:T(512)S(1)}, bf16[512,1152]{1,0:T(8,128)(2,1)S(1)}, bf16[512,1152]{1,0:T(8,128)(2,1)S(1)}) custom-call(f32[1,1]{1,0:T(1,128)} %bitcast.2.scale_hbm, f32[1,1]{1,0:T(1,128)} %bitcast.3.bias_hbm, bf16[512,1152]{1,0:T(8,128)(2,1)} %image_hbm.1, bf16[512,1152]{1,0:T(8,128)(2,1)} %text_hbm.1), custom_call_target="tpu_custom_call" | custom-call | flops 6643777536 | bytes 4718592 | tf_op jit(solution)/shard_map/exchange/pallas_call | solution.py:274
  114.4 1.4 %write.1 = (f32[512]{0:T(512)}, bf16[512,1152]{1,0:T(8,128)(2,1)}, bf16[512,1152]{1,0:T(8,128)(2,1)}) custom-call(f32[512]{0:T(512)S(1)} %get-tuple-element.6.loss, bf16[512,1152]{1,0:T(8,128)(2,1)S(1)} %get-tuple-element.7.image_grad, bf16[512,1152]{1,0:T(8,128)(2,1)S(1)} %get-tuple-element.8.text_grad), custom_call_target="tpu_custom_call" | custom-call | bytes 4718592 | tf_op jit(solution)/shard_map/write/pallas_call | solution.py:313

commit v6 on v4

--- a/solution.py
+++ b/solution.py
@@ -9,11 +9,11 @@
 
 MESH = pl.DeviceIdType.MESH
 PIECE = 128
-TEXT = 128
+TEXT = 256
 PREPARE = 64
 CHUNK = 128
 FINISH = 64
-WRITE = 128
+WRITE = 512
 
 
 def block(index, size, base=0):

time: 116 us -> 116 us (level)
  no operation moved by 1% of the time
where the time goes in v6:
time: 116 us
  Pallas kernels  114 us (98%)
  between operations  1.93 us (2%)
    pallas_call x1, Pallas kernels, local(): pl.pallas_call(functools.partial(exchange, n), out_shape=outs, in_specs=[...  112 us

profile of v6, /device:TPU:122, one launch (start us, length us, event | category | flops | bytes accessed | tf_op | source)
XLA Modules:
  0.0 115.7 jit_solution(13652829122170055234)
XLA Ops:
  1.9 112.4 %exchange.1 = (f32[512]{0:T(512)S(1)}, bf16[512,1152]{1,0:T(8,128)(2,1)S(1)}, bf16[512,1152]{1,0:T(8,128)(2,1)S(1)}) custom-call(f32[1,1]{1,0:T(1,128)} %bitcast.2.scale_hbm, f32[1,1]{1,0:T(1,128)} %bitcast.3.bias_hbm, bf16[512,1152]{1,0:T(8,128)(2,1)} %image_hbm.1, bf16[512,1152]{1,0:T(8,128)(2,1)} %text_hbm.1), custom_call_target="tpu_custom_call" | custom-call | flops 6643777536 | bytes 4718592 | tf_op jit(solution)/shard_map/exchange/pallas_call | solution.py:274
  114.3 1.4 %write.1 = (f32[512]{0:T(512)}, bf16[512,1152]{1,0:T(8,128)(2,1)}, bf16[512,1152]{1,0:T(8,128)(2,1)}) custom-call(f32[512]{0:T(512)S(1)} %get-tuple-element.6.loss, bf16[512,1152]{1,0:T(8,128)(2,1)S(1)} %get-tuple-element.7.image_grad, bf16[512,1152]{1,0:T(8,128)(2,1)S(1)} %get-tuple-element.8.text_grad), custom_call_target="tpu_custom_call" | custom-call | bytes 4718592 | tf_op jit(solution)/shard_map/write/pallas_call | solution.py:313

commit v7 on v4

--- a/solution.py
+++ b/solution.py
@@ -175,11 +175,6 @@
                     preferred_element_type=jnp.float32,
                 ).astype(jnp.bfloat16)
 
-    for side in (0, 1):
-        @pl.loop(0, rows // CHUNK)
-        def _(step):
-            products(side, own, step, diagonal=True)
-
     per = CHUNK // PIECE
     steps = TEXT // CHUNK
 
@@ -198,6 +193,11 @@
         @pl.loop(piece * steps, (piece + 1) * steps)
         def _(step):
             products(0, near, step)
+
+    for side in (0, 1):
+        @pl.loop(0, rows // CHUNK)
+        def _(step):
+            products(side, own, step, diagonal=True)
 
     loss_out[...] = jnp.sum(loss[...].T, axis=0) / (3.0 * rows)
 

time: 116 us -> 116 us (level)
  no operation moved by 1% of the time
where the time goes in v7:
time: 116 us
  Pallas kernels  114 us (98%)
  between operations  1.93 us (2%)
    pallas_call x1, Pallas kernels, local(): pl.pallas_call(functools.partial(exchange, n), out_shape=outs, in_specs=[...  112 us

profile of v7, /device:TPU:122, one launch (start us, length us, event | category | flops | bytes accessed | tf_op | source)
XLA Modules:
  0.0 115.9 jit_solution(4039732644427579405)
XLA Ops:
  1.9 112.5 %exchange.1 = (f32[512]{0:T(512)S(1)}, bf16[512,1152]{1,0:T(8,128)(2,1)S(1)}, bf16[512,1152]{1,0:T(8,128)(2,1)S(1)}) custom-call(f32[1,1]{1,0:T(1,128)} %bitcast.2.scale_hbm, f32[1,1]{1,0:T(1,128)} %bitcast.3.bias_hbm, bf16[512,1152]{1,0:T(8,128)(2,1)} %image_hbm.1, bf16[512,1152]{1,0:T(8,128)(2,1)} %text_hbm.1), custom_call_target="tpu_custom_call" | custom-call | flops 6643777536 | bytes 4718592 | tf_op jit(solution)/shard_map/exchange/pallas_call | solution.py:274
  114.4 1.5 %write.1 = (f32[512]{0:T(512)}, bf16[512,1152]{1,0:T(8,128)(2,1)}, bf16[512,1152]{1,0:T(8,128)(2,1)}) custom-call(f32[512]{0:T(512)S(1)} %get-tuple-element.6.loss, bf16[512,1152]{1,0:T(8,128)(2,1)S(1)} %get-tuple-element.7.image_grad, bf16[512,1152]{1,0:T(8,128)(2,1)S(1)} %get-tuple-element.8.text_grad), custom_call_target="tpu_custom_call" | custom-call | bytes 4718592 | tf_op jit(solution)/shard_map/write/pallas_call | solution.py:313
